TPU v7x, 128 devices: a whole 4x4x4 slice. The times are simulated.
128 devices in a mesh: elem: 8 (over y, core), col: 16 (over x, z).
Axes of the slice: x: 4, y: 4, z: 4, core: 2. Of those that a mesh axis runs over, the one named last changes fastest.
Arguments:
- absorbers: float32 [8, 64, 32768], P(None, None, ('elem', 'col')), may hold values from 0.2 to 5
- cloud_tau: float32 [14, 64, 32768], P(None, None, ('elem', 'col')), may hold values from 0.001 to 0.5
- cloud_ssa: float32 [14, 64, 32768], P(None, None, ('elem', 'col')), may hold values from 0.3 to 0.9
- cloud_asym: float32 [14, 64, 32768], P(None, None, ('elem', 'col')), may hold values from 0.5 to 0.9
- thickness: float32 [64, 32768], P(None, ('elem', 'col')), may hold values from 0.5 to 2
- coszen: float32 [32768], P(('elem', 'col')), may hold values from 0.15 to 1
- albedo: float32 [14, 32768], P(None, ('elem', 'col')), may hold values from 0.05 to 0.8
- sunlit: int32 [32768], P(('elem', 'col')), may hold values from 0 to 1, as said below
- slot_order: int32 [128, 256], P(('elem', 'col')), may hold values from 0 to 255, as said below
- kcoef: float32 [8, 64, 112], replicated, may hold values from 0.02 to 2
- solar: float32 [112], replicated, may hold values from 0.2 to 5
- band_of_g: int32 [112], replicated, may hold values from 0 to 13
Outputs:
- heating: float32 [64, 32768], P(None, ('elem', 'col'))
- surface_down: float32 [32768], P(('elem', 'col'))
Inputs may be any that keep to these rules, and one draw needn't show every extreme that they name: `slot_order`: each row is a permutation of the owner's 256 columns; slot s sends its column to span device s // 2, which places it at d * 2 + s % 2 for owner d. In the span layout given by slot_order, the two span devices of one elem index whose col indices lie half the col axis apart hold exactly 256 sunlit columns together.
All inputs are finite; a program needn't handle non-finite values.
Results may differ from a plain program's by a relative error of at most 0.0003.
Values sent between devices are 32-bit elements; how exact they have to be, the bound alone decides.
A program may use at most 192 MiB of HBM per device.

v0:
```python
import functools
import math

import jax
import jax.numpy as jnp
from jax import lax
from jax.experimental import pallas as pl
from jax.experimental.pallas import tpu as pltpu
from jax.sharding import PartitionSpec as P

MESH = pl.DeviceIdType.MESH
F32 = jnp.float32
BF16 = jnp.bfloat16

NG = 112
NBND = 14
NSP = 8
NLEV = 64
CH = 256
N_ELEM = 8
N_COL = 16
DEVS = 128

WIDE = 128
NARROW = 32
MAIN = WIDE + NARROW
STARTS = (0, 32, 64, 88)
A_CHUNKS = NG // 8
B_CHUNKS = 4
SCALE = 2.0 * math.log2(math.e)


def dot(a, b):
    return jnp.dot(a, b, preferred_element_type=F32)


def iota(shape, axis):
    return lax.broadcasted_iota(jnp.int32, shape, axis)


def one(mask):
    return jnp.where(mask, 1.0, 0.0).astype(BF16)


def halves(x):
    hi = x.astype(BF16)
    return hi, (x - hi.astype(F32)).astype(BF16)


def thirds(x):
    hi = x.astype(BF16)
    rest = x - hi.astype(F32)
    mid = rest.astype(BF16)
    return hi, mid, (rest - mid.astype(F32)).astype(BF16)


def row_times(row, matrix):
    hi, mid, low = thirds(row)
    at = iota((16, row.shape[1]), 0)
    stack = jnp.where(at == 0, hi.astype(F32), jnp.where(at == 1, mid.astype(F32), jnp.where(at == 2, low.astype(F32), 0.0)))
    return jnp.sum(dot(stack.astype(BF16), matrix), axis=0, keepdims=True)


class Tile:
    def __init__(self, first, packed):
        self.first = first
        self.packed = packed
        self.lanes = 2 * WIDE if packed else WIDE
        self.chunks = A_CHUNKS + (B_CHUNKS if packed else 0)

    def compact(self, lane):
        return self.first + jnp.where(lane < WIDE, lane, WIDE + lane % NARROW)


def physics(tile, refs, scr, after_up=None, started=None):
    (ab, ct, cs, ca, th, mu, alb, sun, slot, kc, sol, band) = refs
    (rhs, kt, lhs, buf, state, coef, net, fl, albs) = scr
    lanes, chunks = tile.lanes, tile.chunks

    lit = jnp.where(sun[...] == 1, 1.0, 0.0)
    ri, ci = iota((CH, CH), 0), iota((CH, CH), 1)
    litb = jnp.broadcast_to(lit, (CH, CH))
    ones = jnp.ones((CH, CH), BF16)
    rank_c = dot(jnp.where(ci < ri, litb, 0.0).astype(BF16), ones[:, :lanes])
    lit_c = dot(jnp.where(ci == ri, litb, 0.0).astype(BF16), ones[:, :lanes])
    row_lit = jnp.broadcast_to(lit, (16, CH)).astype(BF16)
    rank_r = dot(row_lit, one(ri < ci))[0:1]
    count = dot(row_lit, ones)[0:1]
    want_c = tile.compact(iota((CH, lanes), 1)).astype(F32)
    gather = one(jnp.where(want_c >= count[:, :lanes], jnp.where(iota((CH, lanes), 0) == 0, 1.0, 0.0), jnp.where(rank_c == want_c, lit_c, 0.0)) > 0.5)
    want_r = tile.compact(iota((lanes, CH), 0)).astype(F32)
    spread = one(jnp.where(rank_r == want_r, jnp.broadcast_to(lit, (lanes, CH)), 0.0) > 0.5)
    to_slot = dot(spread, one(slot[...] == ri)).astype(BF16)

    eye = iota((NG, NG), 0) == iota((NG, NG), 1)
    solar = sol[...]
    weight = jnp.sum(jnp.where(eye, solar / jnp.sum(solar, axis=1, keepdims=True), 0.0), axis=1, keepdims=True)
    band_c = jnp.sum(jnp.where(eye, band[...].astype(F32), 0.0), axis=1, keepdims=True)
    k = iota((NG, CH), 1) % 128
    for l8 in range(8):
        pick = one((k // 8).astype(F32) == jnp.where(k % 8 == l8, band_c, -1.0))
        lhs[l8 // 4, (l8 % 4) * NG:(l8 % 4 + 1) * NG, 256:512] = pick
    for grp in range(8):
        rows = jnp.concatenate([kc[s, 8 * grp:8 * grp + 8, :] for s in range(NSP)], axis=0)
        hi = rows.astype(BF16).astype(F32)
        low = rows - hi
        kt[grp, :, 0:128] = jnp.concatenate([hi, hi], axis=0).T.astype(BF16)
        kt[grp, :, 128:256] = jnp.concatenate([low, low], axis=0).T.astype(BF16)

    quarter = iota((8, WIDE), 1) // NARROW

    def pack(get, j):
        if j == 3:
            return jnp.where(quarter == 0, get(24), get(56))
        v = [get(s + 8 * j) for s in STARTS]
        return jnp.where(quarter == 0, v[0], jnp.where(quarter == 1, v[1], jnp.where(quarter == 2, v[2], v[3])))

    a_hi, a_low = halves(jnp.concatenate([alb[...], jnp.zeros((2, CH), F32)], axis=0))
    zero = jnp.zeros((112, lanes), BF16)
    a_rhs = jnp.concatenate([dot(a_hi, gather).astype(BF16), zero, dot(a_low, gather).astype(BF16), zero], axis=0)
    albs[...] = dot(one(k.astype(F32) == band_c), a_rhs)
    cosine = mu[...]
    cos = row_times(cosine, gather)
    cos_safe = jnp.where(cos > 0, cos, 1.0)
    rate = -0.5 / cos_safe
    wfull = jnp.broadcast_to(weight, (NG, WIDE))

    def lanes_of(x, c):
        return x[:, :WIDE] if c < A_CHUNKS else x[:, WIDE:]

    def chunk_of(c, get):
        if c < A_CHUNKS:
            return get(8 * c, 0)
        return pack(lambda row: get(row, WIDE), c - A_CHUNKS)

    def beam_top(c):
        w = chunk_of(c, lambda row, lane: wfull[row:row + 8])
        if c == A_CHUNKS + 3:
            w = jnp.where(quarter < 2, w, 0.0)
        return w * lanes_of(cos, c)

    for c in range(chunks):
        a = chunk_of(c, lambda row, lane: albs[row:row + 8, lane:lane + WIDE])
        at = slice(8 * c, 8 * c + 8)
        state[0, at] = a
        state[1, at] = a
        state[2, at] = jnp.ones((8, WIDE), F32)
        state[3, at] = jnp.ones((8, WIDE), F32)

    def prepare(grp, _):
        rows = pl.ds(pl.multiple_of(grp * 8, 8), 8)
        thick = th[rows, :] * (SCALE / NLEV)
        gas = (ab[:, rows, :] * thick[None]).reshape(64, CH)
        tau = (ct[:, rows, :] * SCALE).reshape(112, CH)
        tau_s = tau * cs[:, rows, :].reshape(112, CH)
        tau_f = tau_s * ca[:, rows, :].reshape(112, CH)
        hi, low = halves(jnp.concatenate([gas, tau, tau_s, tau_f], axis=0))
        hi = dot(hi, gather).astype(BF16)
        low = dot(low, gather).astype(BF16)
        rhs[grp, 0:64] = hi[0:64]
        rhs[grp, 64:128] = low[0:64]
        rhs[grp, 128:192] = hi[0:64]
        rhs[grp, 192:256] = low[0:64]
        gap = jnp.zeros((16, lanes), BF16)
        for i in range(3):
            at = 64 + 112 * i
            rhs[grp, 256 * i + 256:256 * i + 368] = hi[at:at + 112]
            rhs[grp, 256 * i + 368:256 * i + 384] = gap
            rhs[grp, 256 * i + 384:256 * i + 496] = low[at:at + 112]
            rhs[grp, 256 * i + 496:256 * i + 512] = gap
        return 0

    lax.fori_loop(0, 8, prepare, 0)

    lane8 = iota((NG, CH), 1) % 8

    def optics(grp, hf):
        for j in range(4):
            lhs[hf, j * NG:(j + 1) * NG, 0:256] = jnp.where(lane8 == hf * 4 + j, kt[grp].astype(F32), 0.0).astype(BF16)
        buf[hf, 0] = dot(lhs[hf], rhs[grp, 0:512])
        buf[hf, 1] = dot(lhs[hf, :, 256:512], rhs[grp, 512:768])
        buf[hf, 2] = dot(lhs[hf, :, 256:512], rhs[grp, 768:1024])

    def climb(grp, hf):
        for c in range(chunks):
            at = slice(8 * c, 8 * c + 8)
            a, q, tt, sb = (state[i, at] for i in range(4))
            m, r = lanes_of(cos_safe, c), lanes_of(rate, c)
            for j in (3, 2, 1, 0):
                t, s, f = (chunk_of(c, lambda row, lane: buf[hf, i, j * NG + row:j * NG + row + 8, lane:lane + WIDE]) for i in range(3))
                p1 = t - s
                p2 = t - f
                pp = p1 * p2
                kk = pp * lax.rsqrt(pp)
                e = jnp.exp2(-kk)
                e2 = e * e
                tot = p1 + p2
                k2 = kk + kk
                inv_d = pl.reciprocal((tot + k2) - e2 * (tot - k2), approx=True)
                rdif = (s - f) * (1.0 - e2) * inv_d
                tdif = (k2 + k2) * e * inv_d
                u = jnp.exp2(t * r)
                sc = (1.0 - u) * pl.reciprocal(t + t, approx=True)
                mf = m * f
                rdir = sc * (s - mf)
                tdir = sc * (s + mf)
                inv = pl.reciprocal(1.0 - rdif * a, approx=True)
                ti = tdif * inv
                qu = q * u
                b = (rdif * qu + tdir) * inv
                level = pl.multiple_of((grp * 8 + hf * 4 + j) * (8 * chunks), 8) + 8 * c
                w = pl.ds(pl.multiple_of(level, 8), 8)
                coef[0, w] = ti
                coef[1, w] = b
                coef[2, w] = u
                coef[3, w] = 1.0 - a
                coef[4, w] = 1.0 - q
                sb = tt * b + sb * u
                tt = tt * ti
                q = rdir + ti * (qu + a * tdir)
                a = rdif + tdif * (a * ti)
            state[0, at] = a
            state[1, at] = q
            state[2, at] = tt
            state[3, at] = sb

    optics(7, 1)

    def up(i, _):
        grp = 7 - i
        optics(grp, 0)
        climb(grp, 1)
        optics(jnp.maximum(grp - 1, 0), 1)
        climb(grp, 0)
        return 0

    lax.fori_loop(0, 8, up, 0)

    def side(make):
        parts = [sum(make(c) for c in range(A_CHUNKS))]
        if tile.packed:
            parts.append(sum(make(c) for c in range(A_CHUNKS, chunks)))
        return jnp.concatenate(parts, axis=1)

    beams = [beam_top(c) for c in range(chunks)]
    surf = jnp.sum(side(lambda c: state[3, 8 * c:8 * c + 8] * beams[c]), axis=0, keepdims=True)
    slotted = row_times(surf, to_slot)
    if after_up is not None:
        after_up(slotted)

    net[0:8] = side(lambda c: beams[c] * (1.0 - state[1, 8 * c:8 * c + 8]))
    UNROLL = 4

    def down(i, carry):
        dn, bm = list(carry[0]), list(carry[1])
        for j in range(UNROLL):
            l = i * UNROLL + j
            total = [None, None]
            for c in range(chunks):
                w = pl.ds(pl.multiple_of(l * (8 * chunks) + 8 * c, 8), 8)
                d = coef[0, w] * dn[c] + coef[1, w] * bm[c]
                bb = bm[c] * coef[2, w]
                v = bb * coef[4, w] + d * coef[3, w]
                dn[c], bm[c] = d, bb
                which = 0 if c < A_CHUNKS else 1
                total[which] = v if total[which] is None else total[which] + v
            at = pl.ds(pl.multiple_of(l * 8 + 8, 8), 8)
            net[at, 0:WIDE] = total[0]
            if tile.packed:
                net[at, WIDE:] = total[1]
        return tuple(dn), tuple(bm)

    lax.fori_loop(0, NLEV // UNROLL, down, (tuple(jnp.zeros((8, WIDE), F32) for _ in range(chunks)), tuple(beams)))
    net[8 * 65:8 * 72] = jnp.zeros((56, lanes), F32)
    fl[...] = jnp.sum(net[...].reshape(72, 8, lanes), axis=1)
    hi, mid, low = thirds(fl[0:64] - fl[1:65])
    lost = dot(hi, spread) + dot(mid, spread) + dot(low, spread)
    heat = NLEV * lost / th[...]
    return heat, slotted


def scratch(tile):
    lanes, rows = tile.lanes, 8 * tile.chunks
    return [
        pltpu.VMEM((8, 1024, lanes), BF16),
        pltpu.VMEM((8, NG, 256), BF16),
        pltpu.VMEM((2, 4 * NG, 512), BF16),
        pltpu.VMEM((2, 3, 4 * NG, lanes), F32),
        pltpu.VMEM((4, rows, WIDE), F32),
        pltpu.VMEM((5, NLEV * rows, WIDE), F32),
        pltpu.VMEM((72 * 8, lanes), F32),
        pltpu.VMEM((72, lanes), F32),
        pltpu.VMEM((NG, lanes), F32),
    ]


def overflow_kernel(*refs):
    sun, hbm, (heat, slotted) = refs[0], refs[1:12], refs[12:14]
    local, sem, scr = refs[14:25], refs[25], refs[26:]
    heat[...] = jnp.zeros_like(heat)
    slotted[...] = jnp.zeros_like(slotted)

    @pl.when(jnp.sum(jnp.where(sun[...] == 1, 1, 0)) > MAIN)
    def _():
        for i in range(11):
            copy = pltpu.make_async_copy(hbm[i], local[i], sem.at[i])
            copy.start()
            copy.wait()
        ins = local[:7] + (sun,) + local[7:]
        h, s = physics(Tile(MAIN, False), ins, scr)
        heat[...] = h
        slotted[...] = s


def main_kernel(*refs):
    ins, (heat0, slotted0), (heat, surface) = refs[:12], refs[12:14], refs[14:16]
    send, recv, send_sem, recv_sem, go = refs[16:21]
    scr = refs[21:]
    e, c = lax.axis_index("elem"), lax.axis_index("col")
    me = e * N_COL + c

    barrier = pltpu.get_barrier_semaphore()
    for k in range(1, N_COL):
        pl.semaphore_signal(barrier, inc=1, device_id=(e, lax.rem(c + k, N_COL)), device_id_type=MESH)
    for k in range(1, N_ELEM):
        pl.semaphore_signal(barrier, inc=1, device_id=(lax.rem(e + k, N_ELEM), c), device_id_type=MESH)

    def ship(slotted):
        slotted = slotted + slotted0[...]
        at, s = iota((DEVS, CH), 0), iota((DEVS, CH), 1)
        own = jnp.where(s // 2 == at, slotted, 0.0)
        send[...] = (own[:, :128] + own[:, 128:]).reshape(DEVS, 1, 128)
        pl.semaphore_wait(barrier, N_COL - 1 + N_ELEM - 1)
        for k in range(1, N_ELEM):
            pl.semaphore_signal(go, inc=1, device_id=(lax.rem(e + k, N_ELEM), c), device_id_type=MESH)
        pl.semaphore_wait(go, N_ELEM - 1)
        recv[me] = send[me]

        def push(k, _):
            t = lax.rem(me + k, DEVS)
            pltpu.make_async_remote_copy(
                src_ref=send.at[t],
                dst_ref=recv.at[me],
                send_sem=send_sem,
                recv_sem=recv_sem,
                device_id=(t // N_COL, lax.rem(t, N_COL)),
                device_id_type=MESH,
            ).start()
            return 0

        lax.fori_loop(1, DEVS, push, 0)

    h, _ = physics(Tile(0, True), ins, scr, after_up=ship)
    heat[...] = h + heat0[...]
    rest = recv.at[pl.ds(0, DEVS - 1)]
    pltpu.make_async_copy(rest, rest, recv_sem).wait()
    pltpu.make_async_copy(rest, rest, send_sem).wait()
    got = recv[...].reshape(DEVS, 128)
    lane = iota((DEVS, 128), 1)
    first = lax.rem(2 * me, 128)
    even = jnp.sum(jnp.where(lane == first, got, 0.0), axis=1, keepdims=True)
    odd = jnp.sum(jnp.where(lane == first + 1, got, 0.0), axis=1, keepdims=True)
    at, s = iota((DEVS, CH), 0), iota((DEVS, CH), 1)
    surface[...] = jnp.sum(jnp.where(s // 2 == at, jnp.where(s % 2 == 0, even, odd), 0.0), axis=0, keepdims=True)


def body(*args):
    args = tuple(a.reshape(1, -1) if a.ndim == 1 else a for a in args)
    vmem, hbm = pl.BlockSpec(memory_space=pltpu.VMEM), pl.BlockSpec(memory_space=pl.ANY)
    outs = (jax.ShapeDtypeStruct((NLEV, CH), F32), jax.ShapeDtypeStruct((1, CH), F32))
    rest = args[:7] + args[8:]
    extra = pl.pallas_call(
        overflow_kernel,
        out_shape=outs,
        in_specs=[vmem] + [hbm] * 11,
        out_specs=(vmem, vmem),
        scratch_shapes=[pltpu.VMEM(a.shape, a.dtype) for a in rest] + [pltpu.SemaphoreType.DMA((11,))] + scratch(Tile(MAIN, False)),
        compiler_params=pltpu.CompilerParams(vmem_limit_bytes=60 * 2**20),
    )(args[7], *rest)
    heat, surface = pl.pallas_call(
        main_kernel,
        out_shape=outs,
        in_specs=[vmem] * 14,
        out_specs=(vmem, vmem),
        scratch_shapes=[
            pltpu.VMEM((DEVS, 1, 128), F32),
            pltpu.VMEM((DEVS, 1, 128), F32),
            pltpu.SemaphoreType.DMA,
            pltpu.SemaphoreType.DMA,
            pltpu.SemaphoreType.REGULAR,
        ]
        + scratch(Tile(0, True)),
        compiler_params=pltpu.CompilerParams(vmem_limit_bytes=60 * 2**20, collective_id=0, has_side_effects=True),
    )(*args, *extra)
    return heat, surface.reshape(CH)


def solution(mesh):
    columns = ("elem", "col")
    return jax.shard_map(
        body,
        mesh=mesh,
        in_specs=(
            P(None, None, columns),
            P(None, None, columns),
            P(None, None, columns),
            P(None, None, columns),
            P(None, columns),
            P(columns),
            P(None, columns),
            P(columns),
            P(columns, None),
            P(),
            P(),
            P(),
        ),
        out_specs=(P(None, columns), P(columns)),
        check_vma=False,
    )
```

profile of v0, /device:TPU:1, one launch (start us, length us, event | category | flops | bytes accessed | tf_op | source)
XLA Modules:
  0.0 36.7 jit_solution(6858607860784313821)
XLA Ops:
  0.6 1.5 %shard_map.131 = (f32[64,256]{1,0:T(8,128)}, f32[1,256]{1,0:T(1,128)}) custom-call(s32[1,256]{1,0:T(1,128)} %bitcast.7, f32[8,64,256]{2,1,0:T(8,128)} %refs_0_.1, f32[14,64,256]{2,1,0:T(8,128)} %refs_1_.3, f32[14,64,256]{2,1,0:T(8,128)} %refs_2_.3, f32[14,64,256]{2,1,0:T(8,128)} %refs_3_.3, f32[64,256]{1,0:T(8,128)} %refs_4_.3, f32[1,256]{1,0:T(1,128)} %bitcast.5, ...), custom_call_target="tpu_custom_call" | custom-call | tf_op jit(solution)/shard_map/pallas_call | solution.py:372
  2.2 32.4 %shard_map.132 = (f32[64,256]{1,0:T(8,128)}, f32[1,256]{1,0:T(1,128)}) custom-call(f32[8,64,256]{2,1,0:T(8,128)} %refs_0_.1, f32[14,64,256]{2,1,0:T(8,128)} %refs_1_.3, f32[14,64,256]{2,1,0:T(8,128)} %refs_2_.3, f32[14,64,256]{2,1,0:T(8,128)} %refs_3_.3, f32[64,256]{1,0:T(8,128)} %refs_4_.3, f32[1,256]{1,0:T(1,128)} %bitcast.6, f32[14,256]{1,0:T(8,128)} %refs_6_.1, ...), custom_call_target="tpu_custom_call" | custom-call | tf_op jit(solution)/shard_map/pallas_call | solution.py:380
  34.6 0.0 copy-start
  34.6 1.5 %copy.16 = f32[64,256]{1,0:T(8,128)} copy(f32[64,256]{1,0:T(8,128)} %get-tuple-element.12) | data formatting | bytes 131072
  36.1 0.0 copy-done
  36.1 0.6 %copy.17 = f32[256]{0:T(256)} copy(f32[256]{0:T(256)S(1)} %bitcast.13) | data formatting | bytes 2048
Async XLA Ops:
  34.6 1.5 %copy-start = (f32[1,256]{1,0:T(1,128)S(1)}, f32[1,256]{1,0:T(1,128)}, u32[]{:S(2)}) copy-start(f32[1,256]{1,0:T(1,128)} %get-tuple-element.9) | copy-start | bytes 3076
where the time goes:
time: 36.8 us; the launch traced here: 36.7 us
  Pallas kernels  34 us (92%)
  local copies, waits for them, and re-layouts  2.04 us (6%)
  between operations  0.65 us (2%)
    pallas_call x1, Pallas kernels, body(): pl.pallas_call(main_kernel, out_shape=outs, in_specs=[vmem] * 14, out_spe...  32.4 us
    unnamed x4, local copies, waits for them, and re-layouts  2.04 us
    pallas_call x1, Pallas kernels, body(): pl.pallas_call(overflow_kernel, out_shape=outs, in_specs=[vmem] + [hbm] *...  1.55 us

commit v1 on v0

--- a/solution.py
+++ b/solution.py
@@ -27,7 +27,10 @@
 STARTS = (0, 32, 64, 88)
 A_CHUNKS = NG // 8
 B_CHUNKS = 4
-SCALE = 2.0 * math.log2(math.e)
+SCALE = math.log2(math.e)
+
+
+LIMIT = 56 * 2**20
 
 
 def dot(a, b):
@@ -72,9 +75,9 @@
         return self.first + jnp.where(lane < WIDE, lane, WIDE + lane % NARROW)
 
 
-def physics(tile, refs, scr, after_up=None, started=None):
+def physics(tile, refs, scr, loaded=None, midway=None, after_up=None):
     (ab, ct, cs, ca, th, mu, alb, sun, slot, kc, sol, band) = refs
-    (rhs, kt, lhs, buf, state, coef, net, fl, albs) = scr
+    (rhs, masks, lhs, buf, state, coef, net, fl, albs) = scr
     lanes, chunks = tile.lanes, tile.chunks
 
     lit = jnp.where(sun[...] == 1, 1.0, 0.0)
@@ -100,12 +103,8 @@
     for l8 in range(8):
         pick = one((k // 8).astype(F32) == jnp.where(k % 8 == l8, band_c, -1.0))
         lhs[l8 // 4, (l8 % 4) * NG:(l8 % 4 + 1) * NG, 256:512] = pick
-    for grp in range(8):
-        rows = jnp.concatenate([kc[s, 8 * grp:8 * grp + 8, :] for s in range(NSP)], axis=0)
-        hi = rows.astype(BF16).astype(F32)
-        low = rows - hi
-        kt[grp, :, 0:128] = jnp.concatenate([hi, hi], axis=0).T.astype(BF16)
-        kt[grp, :, 128:256] = jnp.concatenate([low, low], axis=0).T.astype(BF16)
+    for l8 in range(8):
+        masks[l8] = one(iota((16, CH), 1) % 8 == l8)
 
     quarter = iota((8, WIDE), 1) // NARROW
 
@@ -115,14 +114,10 @@
         v = [get(s + 8 * j) for s in STARTS]
         return jnp.where(quarter == 0, v[0], jnp.where(quarter == 1, v[1], jnp.where(quarter == 2, v[2], v[3])))
 
-    a_hi, a_low = halves(jnp.concatenate([alb[...], jnp.zeros((2, CH), F32)], axis=0))
-    zero = jnp.zeros((112, lanes), BF16)
-    a_rhs = jnp.concatenate([dot(a_hi, gather).astype(BF16), zero, dot(a_low, gather).astype(BF16), zero], axis=0)
-    albs[...] = dot(one(k.astype(F32) == band_c), a_rhs)
     cosine = mu[...]
     cos = row_times(cosine, gather)
     cos_safe = jnp.where(cos > 0, cos, 1.0)
-    rate = -0.5 / cos_safe
+    rate = -1.0 / cos_safe
     wfull = jnp.broadcast_to(weight, (NG, WIDE))
 
     def lanes_of(x, c):
@@ -139,15 +134,7 @@
             w = jnp.where(quarter < 2, w, 0.0)
         return w * lanes_of(cos, c)
 
-    for c in range(chunks):
-        a = chunk_of(c, lambda row, lane: albs[row:row + 8, lane:lane + WIDE])
-        at = slice(8 * c, 8 * c + 8)
-        state[0, at] = a
-        state[1, at] = a
-        state[2, at] = jnp.ones((8, WIDE), F32)
-        state[3, at] = jnp.ones((8, WIDE), F32)
-
-    def prepare(grp, _):
+    def prepare(grp):
         rows = pl.ds(pl.multiple_of(grp * 8, 8), 8)
         thick = th[rows, :] * (SCALE / NLEV)
         gas = (ab[:, rows, :] * thick[None]).reshape(64, CH)
@@ -157,29 +144,32 @@
         hi, low = halves(jnp.concatenate([gas, tau, tau_s, tau_f], axis=0))
         hi = dot(hi, gather).astype(BF16)
         low = dot(low, gather).astype(BF16)
-        rhs[grp, 0:64] = hi[0:64]
-        rhs[grp, 64:128] = low[0:64]
-        rhs[grp, 128:192] = hi[0:64]
-        rhs[grp, 192:256] = low[0:64]
-        gap = jnp.zeros((16, lanes), BF16)
+        rhs[0:64] = hi[0:64]
+        rhs[64:128] = low[0:64]
+        rhs[128:192] = hi[0:64]
+        rhs[192:256] = low[0:64]
         for i in range(3):
             at = 64 + 112 * i
-            rhs[grp, 256 * i + 256:256 * i + 368] = hi[at:at + 112]
-            rhs[grp, 256 * i + 368:256 * i + 384] = gap
-            rhs[grp, 256 * i + 384:256 * i + 496] = low[at:at + 112]
-            rhs[grp, 256 * i + 496:256 * i + 512] = gap
-        return 0
-
-    lax.fori_loop(0, 8, prepare, 0)
-
-    lane8 = iota((NG, CH), 1) % 8
-
-    def optics(grp, hf):
-        for j in range(4):
-            lhs[hf, j * NG:(j + 1) * NG, 0:256] = jnp.where(lane8 == hf * 4 + j, kt[grp].astype(F32), 0.0).astype(BF16)
-        buf[hf, 0] = dot(lhs[hf], rhs[grp, 0:512])
-        buf[hf, 1] = dot(lhs[hf, :, 256:512], rhs[grp, 512:768])
-        buf[hf, 2] = dot(lhs[hf, :, 256:512], rhs[grp, 768:1024])
+            rhs[256 * i + 256:256 * i + 368] = hi[at:at + 112]
+            rhs[256 * i + 384:256 * i + 496] = low[at:at + 112]
+        k_rows = kc[:, rows, :].reshape(64, NG)
+        k_hi = k_rows.astype(BF16).astype(F32)
+        k_low = k_rows - k_hi
+        k_t = jnp.concatenate(
+            [jnp.concatenate([v, v], axis=0).T.astype(BF16) for v in (k_hi, k_low)], axis=1
+        )
+        for l8 in range(8):
+            at = (l8 % 4) * NG
+            lhs[l8 // 4, at:at + NG, 0:256] = k_t * jnp.concatenate([masks[l8]] * 7, axis=0)
+
+    for i in range(3):
+        rhs[256 * i + 368:256 * i + 384] = jnp.zeros((16, lanes), BF16)
+        rhs[256 * i + 496:256 * i + 512] = jnp.zeros((16, lanes), BF16)
+
+    def optics(hf):
+        buf[hf, 0] = dot(lhs[hf], rhs[0:512])
+        buf[hf, 1] = dot(lhs[hf, :, 256:512], rhs[512:768])
+        buf[hf, 2] = dot(lhs[hf, :, 256:512], rhs[768:1024])
 
     def climb(grp, hf):
         for c in range(chunks):
@@ -192,13 +182,13 @@
                 p2 = t - f
                 pp = p1 * p2
                 kk = pp * lax.rsqrt(pp)
-                e = jnp.exp2(-kk)
+                nk2 = kk * -2.0
+                e = jnp.exp2(nk2)
                 e2 = e * e
                 tot = p1 + p2
-                k2 = kk + kk
-                inv_d = pl.reciprocal((tot + k2) - e2 * (tot - k2), approx=True)
+                inv_d = pl.reciprocal((tot - nk2) - e2 * (tot + nk2), approx=True)
                 rdif = (s - f) * (1.0 - e2) * inv_d
-                tdif = (k2 + k2) * e * inv_d
+                tdif = (kk * 4.0) * e * inv_d
                 u = jnp.exp2(t * r)
                 sc = (1.0 - u) * pl.reciprocal(t + t, approx=True)
                 mf = m * f
@@ -224,13 +214,32 @@
             state[2, at] = tt
             state[3, at] = sb
 
-    optics(7, 1)
+    if loaded is not None:
+        loaded(0)
+    a_hi, a_low = halves(jnp.concatenate([alb[...], jnp.zeros((2, CH), F32)], axis=0))
+    zero = jnp.zeros((112, lanes), BF16)
+    a_rhs = jnp.concatenate([dot(a_hi, gather).astype(BF16), zero, dot(a_low, gather).astype(BF16), zero], axis=0)
+    albs[...] = dot(one(k.astype(F32) == band_c), a_rhs)
+    for c in range(chunks):
+        a = chunk_of(c, lambda row, lane: albs[row:row + 8, lane:lane + WIDE])
+        at = slice(8 * c, 8 * c + 8)
+        state[0, at] = a
+        state[1, at] = a
+        state[2, at] = jnp.ones((8, WIDE), F32)
+        state[3, at] = jnp.ones((8, WIDE), F32)
+    prepare(7)
+    optics(1)
+    if loaded is not None:
+        loaded(1)
 
     def up(i, _):
         grp = 7 - i
-        optics(grp, 0)
+        if midway is not None:
+            pl.when(i == 5)(midway)
+        optics(0)
         climb(grp, 1)
-        optics(jnp.maximum(grp - 1, 0), 1)
+        prepare(jnp.maximum(grp - 1, 0))
+        optics(1)
         climb(grp, 0)
         return 0
 
@@ -282,8 +291,8 @@
 def scratch(tile):
     lanes, rows = tile.lanes, 8 * tile.chunks
     return [
-        pltpu.VMEM((8, 1024, lanes), BF16),
-        pltpu.VMEM((8, NG, 256), BF16),
+        pltpu.VMEM((1024, lanes), BF16),
+        pltpu.VMEM((8, 16, 256), BF16),
         pltpu.VMEM((2, 4 * NG, 512), BF16),
         pltpu.VMEM((2, 3, 4 * NG, lanes), F32),
         pltpu.VMEM((4, rows, WIDE), F32),
@@ -295,12 +304,10 @@
 
 
 def overflow_kernel(*refs):
-    sun, hbm, (heat, slotted) = refs[0], refs[1:12], refs[12:14]
-    local, sem, scr = refs[14:25], refs[25], refs[26:]
-    heat[...] = jnp.zeros_like(heat)
-    slotted[...] = jnp.zeros_like(slotted)
-
-    @pl.when(jnp.sum(jnp.where(sun[...] == 1, 1, 0)) > MAIN)
+    sun, hbm, outs = refs[0], refs[1:12], refs[12:14]
+    local, vals, sem, scr = refs[14:25], refs[25:27], refs[27], refs[28:]
+
+    @pl.when(jnp.sum(jnp.where(sun[...] == 1, 1.0, 0.0)) > MAIN)
     def _():
         for i in range(11):
             copy = pltpu.make_async_copy(hbm[i], local[i], sem.at[i])
@@ -308,16 +315,39 @@
             copy.wait()
         ins = local[:7] + (sun,) + local[7:]
         h, s = physics(Tile(MAIN, False), ins, scr)
-        heat[...] = h
-        slotted[...] = s
+        vals[0][...] = h
+        vals[1][...] = s
+        for i in range(2):
+            copy = pltpu.make_async_copy(vals[i], outs[i], sem.at[11 + i])
+            copy.start()
+            copy.wait()
 
 
 def main_kernel(*refs):
-    ins, (heat0, slotted0), (heat, surface) = refs[:12], refs[12:14], refs[14:16]
-    send, recv, send_sem, recv_sem, go = refs[16:21]
-    scr = refs[21:]
+    big, (mu, alb_hbm, sun, slot, kc_hbm, sol, band) = refs[:5], refs[5:12]
+    heat0_hbm, slotted0, (heat, surface) = refs[12], refs[13], refs[14:16]
+    send, recv, heat0, send_sem, recv_sem, go, in_sem = refs[16:23]
+    local, alb, kc, scr = refs[23:28], refs[28], refs[29], refs[30:]
+    small = (mu, alb, sun, slot, kc, sol, band)
     e, c = lax.axis_index("elem"), lax.axis_index("col")
     me = e * N_COL + c
+
+    def pieces(first):
+        got = []
+        for i in range(5):
+            rows = pl.ds(NLEV - 8, 8) if first else pl.ds(0, NLEV - 8)
+            src, dst = (r.at[rows] if i == 4 else r.at[:, rows] for r in (big[i], local[i]))
+            got.append(pltpu.make_async_copy(src, dst, in_sem.at[i if first else 5 + i]))
+        if first:
+            got.append(pltpu.make_async_copy(alb_hbm, alb, in_sem.at[11]))
+            got.append(pltpu.make_async_copy(kc_hbm, kc, in_sem.at[12]))
+        else:
+            got.append(pltpu.make_async_copy(heat0_hbm, heat0, in_sem.at[10]))
+        return got
+
+    for first in (True, False):
+        for copy in pieces(first):
+            copy.start()
 
     barrier = pltpu.get_barrier_semaphore()
     for k in range(1, N_COL):
@@ -325,36 +355,38 @@
     for k in range(1, N_ELEM):
         pl.semaphore_signal(barrier, inc=1, device_id=(lax.rem(e + k, N_ELEM), c), device_id_type=MESH)
 
+    def loaded(part):
+        for copy in pieces(part == 0):
+            copy.wait()
+
+    def midway():
+        pl.semaphore_wait(barrier, N_COL - 1 + N_ELEM - 1)
+        for k in range(1, N_ELEM):
+            pl.semaphore_signal(go, inc=1, device_id=(lax.rem(e + k, N_ELEM), c), device_id_type=MESH)
+
+    many = jnp.sum(jnp.where(sun[...] == 1, 1.0, 0.0), axis=1, keepdims=True) > MAIN
+
     def ship(slotted):
-        slotted = slotted + slotted0[...]
+        slotted = slotted + jnp.where(many, slotted0[...], 0.0)
         at, s = iota((DEVS, CH), 0), iota((DEVS, CH), 1)
         own = jnp.where(s // 2 == at, slotted, 0.0)
         send[...] = (own[:, :128] + own[:, 128:]).reshape(DEVS, 1, 128)
-        pl.semaphore_wait(barrier, N_COL - 1 + N_ELEM - 1)
-        for k in range(1, N_ELEM):
-            pl.semaphore_signal(go, inc=1, device_id=(lax.rem(e + k, N_ELEM), c), device_id_type=MESH)
         pl.semaphore_wait(go, N_ELEM - 1)
-        recv[me] = send[me]
-
-        def push(k, _):
-            t = lax.rem(me + k, DEVS)
+        for te, tc in farthest_first(e, c):
             pltpu.make_async_remote_copy(
-                src_ref=send.at[t],
+                src_ref=send.at[te * N_COL + tc],
                 dst_ref=recv.at[me],
                 send_sem=send_sem,
                 recv_sem=recv_sem,
-                device_id=(t // N_COL, lax.rem(t, N_COL)),
+                device_id=(te, tc),
                 device_id_type=MESH,
             ).start()
-            return 0
-
-        lax.fori_loop(1, DEVS, push, 0)
-
-    h, _ = physics(Tile(0, True), ins, scr, after_up=ship)
-    heat[...] = h + heat0[...]
+        recv[me] = send[me]
+
+    h, _ = physics(Tile(0, True), local + small, scr, loaded=loaded, midway=midway, after_up=ship)
+    heat[...] = h + jnp.where(many, heat0[...], 0.0)
     rest = recv.at[pl.ds(0, DEVS - 1)]
     pltpu.make_async_copy(rest, rest, recv_sem).wait()
-    pltpu.make_async_copy(rest, rest, send_sem).wait()
     got = recv[...].reshape(DEVS, 128)
     lane = iota((DEVS, 128), 1)
     first = lax.rem(2 * me, 128)
@@ -362,35 +394,55 @@
     odd = jnp.sum(jnp.where(lane == first + 1, got, 0.0), axis=1, keepdims=True)
     at, s = iota((DEVS, CH), 0), iota((DEVS, CH), 1)
     surface[...] = jnp.sum(jnp.where(s // 2 == at, jnp.where(s % 2 == 0, even, odd), 0.0), axis=0, keepdims=True)
+    pltpu.make_async_copy(rest, rest, send_sem).wait()
+
+
+def farthest_first(e, c):
+    y, core, x, z = e // 2, lax.rem(e, 2), c // 4, lax.rem(c, 4)
+    ys = [lax.rem(y + i, 4) * 2 for i in range(4)]
+    cores = [core, 1 - core]
+    xs = [lax.rem(x + i, 4) * 4 for i in range(4)]
+    zs = [lax.rem(z + i, 4) for i in range(4)]
+    elems = {(i, j): ys[i] + cores[j] for i in range(4) for j in range(2)}
+    cols = {(i, j): xs[i] + zs[j] for i in range(4) for j in range(4)}
+    hops = (0, 1, 2, 1)
+    steps = [(i, j, k, m) for i in range(4) for j in range(2) for k in range(4) for m in range(4)][1:]
+    steps.sort(key=lambda d: (-(hops[d[0]] + hops[d[2]] + hops[d[3]]), -d[1]))
+    return [(elems[d[0], d[1]], cols[d[2], d[3]]) for d in steps]
 
 
 def body(*args):
     args = tuple(a.reshape(1, -1) if a.ndim == 1 else a for a in args)
-    vmem, hbm = pl.BlockSpec(memory_space=pltpu.VMEM), pl.BlockSpec(memory_space=pl.ANY)
+    vmem, hbm = pl.BlockSpec(memory_space=pltpu.VMEM), pl.BlockSpec(memory_space=pltpu.HBM)
     outs = (jax.ShapeDtypeStruct((NLEV, CH), F32), jax.ShapeDtypeStruct((1, CH), F32))
     rest = args[:7] + args[8:]
     extra = pl.pallas_call(
         overflow_kernel,
         out_shape=outs,
         in_specs=[vmem] + [hbm] * 11,
-        out_specs=(vmem, vmem),
-        scratch_shapes=[pltpu.VMEM(a.shape, a.dtype) for a in rest] + [pltpu.SemaphoreType.DMA((11,))] + scratch(Tile(MAIN, False)),
-        compiler_params=pltpu.CompilerParams(vmem_limit_bytes=60 * 2**20),
+        out_specs=(hbm, hbm),
+        scratch_shapes=[pltpu.VMEM(a.shape, a.dtype) for a in rest]
+        + [pltpu.VMEM((NLEV, CH), F32), pltpu.VMEM((1, CH), F32), pltpu.SemaphoreType.DMA((13,))]
+        + scratch(Tile(MAIN, False)),
+        compiler_params=pltpu.CompilerParams(vmem_limit_bytes=LIMIT),
     )(args[7], *rest)
     heat, surface = pl.pallas_call(
         main_kernel,
-        out_shape=outs,
-        in_specs=[vmem] * 14,
+        out_shape=(pltpu.VMEM((NLEV, CH), F32), pltpu.VMEM((1, CH), F32)),
+        in_specs=[hbm] * 5 + [vmem, hbm, vmem, vmem, hbm, vmem, vmem] + [hbm, vmem],
         out_specs=(vmem, vmem),
         scratch_shapes=[
             pltpu.VMEM((DEVS, 1, 128), F32),
             pltpu.VMEM((DEVS, 1, 128), F32),
+            pltpu.VMEM((NLEV, CH), F32),
             pltpu.SemaphoreType.DMA,
             pltpu.SemaphoreType.DMA,
             pltpu.SemaphoreType.REGULAR,
+            pltpu.SemaphoreType.DMA((13,)),
         ]
+        + [pltpu.VMEM(a.shape, a.dtype) for a in args[:5] + (args[6], args[9])]
         + scratch(Tile(0, True)),
-        compiler_params=pltpu.CompilerParams(vmem_limit_bytes=60 * 2**20, collective_id=0, has_side_effects=True),
+        compiler_params=pltpu.CompilerParams(vmem_limit_bytes=LIMIT, collective_id=0, has_side_effects=True),
     )(*args, *extra)
     return heat, surface.reshape(CH)
 

time: 36.8 us -> 30.7 us (0.83)
  Pallas kernels: 34 us -> 28.7 us
  local copies, waits for them, and re-layouts: 2.04 us -> 1.19 us
    pallas_call x1, Pallas kernels: 32.4 us -> 27.8 us  [body(): pl.pallas_call(main_kernel, out_shape=(pltpu.VMEM((NLEV, CH), F32), pltpu...]
    unnamed x4 -> x2, local copies, waits for them, and re-layouts: 2.04 us -> 1.19 us
    pallas_call x1, Pallas kernels: 1.55 us -> 0.93 us  [body(): pl.pallas_call(overflow_kernel, out_shape=outs, in_specs=[vmem] + [hbm] *...]
where the time goes in v1:
time: 30.7 us; the launch traced here: 30.6 us
  Pallas kernels  28.7 us (93%)
  local copies, waits for them, and re-layouts  1.19 us (4%)
  between operations  0.65 us (2%)
    pallas_call x1, Pallas kernels, body(): pl.pallas_call(main_kernel, out_shape=(pltpu.VMEM((NLEV, CH), F32), pltpu...  27.8 us
    unnamed x2, local copies, waits for them, and re-layouts  1.19 us
    pallas_call x1, Pallas kernels, body(): pl.pallas_call(overflow_kernel, out_shape=outs, in_specs=[vmem] + [hbm] *...  0.93 us

profile of v1, /device:TPU:1, one launch (start us, length us, event | category | flops | bytes accessed | tf_op | source)
XLA Modules:
  0.0 30.6 jit_solution(11501840935688976292)
XLA Ops:
  0.6 0.9 %shard_map.131 = (f32[64,256]{1,0:T(8,128)}, f32[1,256]{1,0:T(1,128)}) custom-call(s32[1,256]{1,0:T(1,128)} %bitcast.8, f32[8,64,256]{2,1,0:T(8,128)} %refs_0_.1, f32[14,64,256]{2,1,0:T(8,128)} %refs_1_.3, f32[14,64,256]{2,1,0:T(8,128)} %refs_2_.3, f32[14,64,256]{2,1,0:T(8,128)} %refs_3_.3, f32[64,256]{1,0:T(8,128)} %refs_4_.3, f32[1,256]{1,0:T(1,128)} %bitcast.6, ...), custom_call_target="tpu_custom_call" | custom-call | tf_op jit(solution)/shard_map/pallas_call | solution.py:419
  1.6 27.8 %shard_map.132 = (f32[64,256]{1,0:T(8,128)S(1)}, f32[1,256]{1,0:T(1,128)S(1)}) custom-call(f32[8,64,256]{2,1,0:T(8,128)} %refs_0_.1, f32[14,64,256]{2,1,0:T(8,128)} %refs_1_.3, f32[14,64,256]{2,1,0:T(8,128)} %refs_2_.3, f32[14,64,256]{2,1,0:T(8,128)} %refs_3_.3, f32[64,256]{1,0:T(8,128)} %refs_4_.3, f32[1,256]{1,0:T(1,128)} %bitcast.7, f32[14,256]{1,0:T(8,128)} %refs_6_.1, ...), custom_call_target="tpu_custom_call" | custom-call | tf_op jit(solution)/shard_map/pallas_call | solution.py:429
  29.4 0.6 %copy.16 = f32[64,256]{1,0:T(8,128)} copy(f32[64,256]{1,0:T(8,128)S(1)} %get-tuple-element.10) | data formatting | bytes 131072
  30.0 0.6 %copy.17 = f32[256]{0:T(256)} copy(f32[256]{0:T(256)S(1)} %bitcast.5) | data formatting | bytes 2048

commit v2 on v1

--- a/solution.py
+++ b/solution.py
@@ -75,9 +75,9 @@
         return self.first + jnp.where(lane < WIDE, lane, WIDE + lane % NARROW)
 
 
-def physics(tile, refs, scr, loaded=None, midway=None, after_up=None):
+def physics(tile, refs, scr, loaded=None, midway=None, after_down=None):
     (ab, ct, cs, ca, th, mu, alb, sun, slot, kc, sol, band) = refs
-    (rhs, masks, lhs, buf, state, coef, net, fl, albs) = scr
+    (rhs, taus, masks, mixed, lhs, buf, state, coef, net, fl, albs) = scr
     lanes, chunks = tile.lanes, tile.chunks
 
     lit = jnp.where(sun[...] == 1, 1.0, 0.0)
@@ -103,8 +103,15 @@
     for l8 in range(8):
         pick = one((k // 8).astype(F32) == jnp.where(k % 8 == l8, band_c, -1.0))
         lhs[l8 // 4, (l8 % 4) * NG:(l8 % 4 + 1) * NG, 256:512] = pick
-    for l8 in range(8):
-        masks[l8] = one(iota((16, CH), 1) % 8 == l8)
+    k4 = iota((NG, CH), 1) - 96
+    k4 = jnp.where(k4 >= 56, k4 - 56, k4)
+    b4 = jnp.where(iota((NG, CH), 1) < 96, -2.0, (k4 // 4).astype(F32))
+    for j in range(4):
+        masks[j] = one(iota((16, 128), 1) % 4 == j)
+        pick = one(b4 == jnp.where(k4 % 4 == j, band_c, -1.0))
+        mixed[j] = pick[:, 0:128]
+        for hf in range(2):
+            lhs[hf, j * NG:(j + 1) * NG, 128:256] = pick[:, 128:256]
 
     quarter = iota((8, WIDE), 1) // NARROW
 
@@ -132,7 +139,7 @@
         w = chunk_of(c, lambda row, lane: wfull[row:row + 8])
         if c == A_CHUNKS + 3:
             w = jnp.where(quarter < 2, w, 0.0)
-        return w * lanes_of(cos, c)
+        return w * lanes_of(cos, c) * 0.5
 
     def prepare(grp):
         rows = pl.ds(pl.multiple_of(grp * 8, 8), 8)
@@ -142,41 +149,45 @@
         tau_s = tau * cs[:, rows, :].reshape(112, CH)
         tau_f = tau_s * ca[:, rows, :].reshape(112, CH)
         hi, low = halves(jnp.concatenate([gas, tau, tau_s, tau_f], axis=0))
-        hi = dot(hi, gather).astype(BF16)
-        low = dot(low, gather).astype(BF16)
-        rhs[0:64] = hi[0:64]
-        rhs[64:128] = low[0:64]
-        rhs[128:192] = hi[0:64]
-        rhs[192:256] = low[0:64]
-        for i in range(3):
-            at = 64 + 112 * i
-            rhs[256 * i + 256:256 * i + 368] = hi[at:at + 112]
-            rhs[256 * i + 384:256 * i + 496] = low[at:at + 112]
+        hi = dot(hi, gather)
+        low = dot(low, gather)
+        hi_f, low_f = hi, low
+        for i in range(2):
+            at = 176 + 112 * i
+            rhs[256 * i:256 * i + 112] = hi_f[at:at + 112].astype(BF16)
+            rhs[256 * i + 128:256 * i + 240] = low_f[at:at + 112].astype(BF16)
         k_rows = kc[:, rows, :].reshape(64, NG)
         k_hi = k_rows.astype(BF16).astype(F32)
         k_low = k_rows - k_hi
-        k_t = jnp.concatenate(
-            [jnp.concatenate([v, v], axis=0).T.astype(BF16) for v in (k_hi, k_low)], axis=1
-        )
-        for l8 in range(8):
-            at = (l8 % 4) * NG
-            lhs[l8 // 4, at:at + NG, 0:256] = k_t * jnp.concatenate([masks[l8]] * 7, axis=0)
-
-    for i in range(3):
-        rhs[256 * i + 368:256 * i + 384] = jnp.zeros((16, lanes), BF16)
-        rhs[256 * i + 496:256 * i + 512] = jnp.zeros((16, lanes), BF16)
+
+        def four(x, count, hf):
+            return jnp.concatenate([x[8 * i + 4 * hf:8 * i + 4 * hf + 4] for i in range(count)], axis=0)
+
+        for hf in range(2):
+            g_hi, g_low = four(hi_f, 8, hf), four(low_f, 8, hf)
+            c_hi, c_low = four(hi_f[64:176], 14, hf), four(low_f[64:176], 14, hf)
+            taus[hf] = jnp.concatenate([g_hi, g_low, g_hi, c_hi, c_low, jnp.zeros((48, lanes), F32)], axis=0).astype(BF16)
+            kh, kl = four(k_hi, 8, hf), four(k_low, 8, hf)
+            k_t = jnp.concatenate([kh, kh, kl, jnp.zeros((32, NG), F32)], axis=0).T.astype(BF16)
+            for j in range(4):
+                at = j * NG
+                lhs[hf, at:at + NG, 0:128] = k_t * jnp.concatenate([masks[j]] * 7, axis=0) + mixed[j]
+
+    for i in range(2):
+        rhs[256 * i + 112:256 * i + 128] = jnp.zeros((16, lanes), BF16)
+        rhs[256 * i + 240:256 * i + 256] = jnp.zeros((16, lanes), BF16)
 
     def optics(hf):
-        buf[hf, 0] = dot(lhs[hf], rhs[0:512])
-        buf[hf, 1] = dot(lhs[hf, :, 256:512], rhs[512:768])
-        buf[hf, 2] = dot(lhs[hf, :, 256:512], rhs[768:1024])
-
-    def climb(grp, hf):
+        buf[hf, 0] = dot(lhs[hf, :, 0:256], taus[hf])
+        buf[hf, 1] = dot(lhs[hf, :, 256:512], rhs[0:256])
+        buf[hf, 2] = dot(lhs[hf, :, 256:512], rhs[256:512])
+
+    def descend(grp, hf):
         for c in range(chunks):
             at = slice(8 * c, 8 * c + 8)
-            a, q, tt, sb = (state[i, at] for i in range(4))
+            refl, diff, beam = (state[i, at] for i in range(3))
             m, r = lanes_of(cos_safe, c), lanes_of(rate, c)
-            for j in (3, 2, 1, 0):
+            for j in range(4):
                 t, s, f = (chunk_of(c, lambda row, lane: buf[hf, i, j * NG + row:j * NG + row + 8, lane:lane + WIDE]) for i in range(3))
                 p1 = t - s
                 p2 = t - f
@@ -189,30 +200,27 @@
                 inv_d = pl.reciprocal((tot - nk2) - e2 * (tot + nk2), approx=True)
                 rdif = (s - f) * (1.0 - e2) * inv_d
                 tdif = (kk * 4.0) * e * inv_d
-                u = jnp.exp2(t * r)
-                sc = (1.0 - u) * pl.reciprocal(t + t, approx=True)
+                below = beam * jnp.exp2(t * r)
+                sc = (beam - below) * pl.reciprocal(t, approx=True)
                 mf = m * f
-                rdir = sc * (s - mf)
-                tdir = sc * (s + mf)
-                inv = pl.reciprocal(1.0 - rdif * a, approx=True)
+                s_up = sc * (s - mf)
+                s_dn = sc * (s + mf)
+                inv = pl.reciprocal(1.0 - rdif * refl, approx=True)
                 ti = tdif * inv
-                qu = q * u
-                b = (rdif * qu + tdir) * inv
                 level = pl.multiple_of((grp * 8 + hf * 4 + j) * (8 * chunks), 8) + 8 * c
                 w = pl.ds(pl.multiple_of(level, 8), 8)
                 coef[0, w] = ti
-                coef[1, w] = b
-                coef[2, w] = u
-                coef[3, w] = 1.0 - a
-                coef[4, w] = 1.0 - q
-                sb = tt * b + sb * u
-                tt = tt * ti
-                q = rdir + ti * (qu + a * tdir)
-                a = rdif + tdif * (a * ti)
-            state[0, at] = a
-            state[1, at] = q
-            state[2, at] = tt
-            state[3, at] = sb
+                coef[1, w] = refl
+                coef[2, w] = diff
+                coef[3, w] = s_up
+                coef[4, w] = rdif * inv
+                coef[5, w] = beam
+                diff = s_dn + ti * (diff + refl * s_up)
+                refl = rdif + tdif * (refl * ti)
+                beam = below
+            state[0, at] = refl
+            state[1, at] = diff
+            state[2, at] = beam
 
     if loaded is not None:
         loaded(0)
@@ -221,29 +229,27 @@
     a_rhs = jnp.concatenate([dot(a_hi, gather).astype(BF16), zero, dot(a_low, gather).astype(BF16), zero], axis=0)
     albs[...] = dot(one(k.astype(F32) == band_c), a_rhs)
     for c in range(chunks):
-        a = chunk_of(c, lambda row, lane: albs[row:row + 8, lane:lane + WIDE])
         at = slice(8 * c, 8 * c + 8)
-        state[0, at] = a
-        state[1, at] = a
-        state[2, at] = jnp.ones((8, WIDE), F32)
-        state[3, at] = jnp.ones((8, WIDE), F32)
-    prepare(7)
-    optics(1)
+        state[0, at] = jnp.zeros((8, WIDE), F32)
+        state[1, at] = jnp.zeros((8, WIDE), F32)
+        state[2, at] = beam_top(c)
+    prepare(0)
+    optics(0)
     if loaded is not None:
         loaded(1)
 
-    def up(i, _):
-        grp = 7 - i
+    def downward(i, _):
+        grp = i
         if midway is not None:
             pl.when(i == 5)(midway)
+        optics(1)
+        descend(grp, 0)
+        prepare(jnp.minimum(grp + 1, 7))
         optics(0)
-        climb(grp, 1)
-        prepare(jnp.maximum(grp - 1, 0))
-        optics(1)
-        climb(grp, 0)
+        descend(grp, 1)
         return 0
 
-    lax.fori_loop(0, 8, up, 0)
+    lax.fori_loop(0, 8, downward, 0)
 
     def side(make):
         parts = [sum(make(c) for c in range(A_CHUNKS))]
@@ -251,35 +257,41 @@
             parts.append(sum(make(c) for c in range(A_CHUNKS, chunks)))
         return jnp.concatenate(parts, axis=1)
 
-    beams = [beam_top(c) for c in range(chunks)]
-    surf = jnp.sum(side(lambda c: state[3, 8 * c:8 * c + 8] * beams[c]), axis=0, keepdims=True)
+    flux, ups = [], []
+    for c in range(chunks):
+        refl, diff, beam = (state[i, 8 * c:8 * c + 8] for i in range(3))
+        al = chunk_of(c, lambda row, lane: albs[row:row + 8, lane:lane + WIDE])
+        beam = beam + beam
+        back = refl * al
+        flux.append(beam + (diff + back * beam) * pl.reciprocal(1.0 - back, approx=True))
+        ups.append(al * flux[-1])
+    surf = jnp.sum(side(lambda c: flux[c]), axis=0, keepdims=True)
     slotted = row_times(surf, to_slot)
-    if after_up is not None:
-        after_up(slotted)
-
-    net[0:8] = side(lambda c: beams[c] * (1.0 - state[1, 8 * c:8 * c + 8]))
+    if after_down is not None:
+        after_down(slotted)
+
+    net[8 * NLEV:8 * NLEV + 8] = side(lambda c: flux[c] - ups[c])
     UNROLL = 4
 
-    def down(i, carry):
-        dn, bm = list(carry[0]), list(carry[1])
+    def rise(i, carry):
+        up_flux = list(carry)
         for j in range(UNROLL):
-            l = i * UNROLL + j
+            l = NLEV - 1 - (i * UNROLL + j)
             total = [None, None]
             for c in range(chunks):
                 w = pl.ds(pl.multiple_of(l * (8 * chunks) + 8 * c, 8), 8)
-                d = coef[0, w] * dn[c] + coef[1, w] * bm[c]
-                bb = bm[c] * coef[2, w]
-                v = bb * coef[4, w] + d * coef[3, w]
-                dn[c], bm[c] = d, bb
+                ti, refl, diff, s_up, ri, beam = (coef[k, w] for k in range(6))
+                up_flux[c] = ti * up_flux[c] + (ri * (diff + refl * s_up) + s_up)
+                v = (beam + beam) + ((diff + refl * up_flux[c]) - up_flux[c])
                 which = 0 if c < A_CHUNKS else 1
                 total[which] = v if total[which] is None else total[which] + v
-            at = pl.ds(pl.multiple_of(l * 8 + 8, 8), 8)
+            at = pl.ds(pl.multiple_of(l * 8, 8), 8)
             net[at, 0:WIDE] = total[0]
             if tile.packed:
                 net[at, WIDE:] = total[1]
-        return tuple(dn), tuple(bm)
-
-    lax.fori_loop(0, NLEV // UNROLL, down, (tuple(jnp.zeros((8, WIDE), F32) for _ in range(chunks)), tuple(beams)))
+        return tuple(up_flux)
+
+    lax.fori_loop(0, NLEV // UNROLL, rise, tuple(ups))
     net[8 * 65:8 * 72] = jnp.zeros((56, lanes), F32)
     fl[...] = jnp.sum(net[...].reshape(72, 8, lanes), axis=1)
     hi, mid, low = thirds(fl[0:64] - fl[1:65])
@@ -291,12 +303,14 @@
 def scratch(tile):
     lanes, rows = tile.lanes, 8 * tile.chunks
     return [
-        pltpu.VMEM((1024, lanes), BF16),
-        pltpu.VMEM((8, 16, 256), BF16),
+        pltpu.VMEM((512, lanes), BF16),
+        pltpu.VMEM((2, 256, lanes), BF16),
+        pltpu.VMEM((4, 16, 128), BF16),
+        pltpu.VMEM((4, NG, 128), BF16),
         pltpu.VMEM((2, 4 * NG, 512), BF16),
         pltpu.VMEM((2, 3, 4 * NG, lanes), F32),
-        pltpu.VMEM((4, rows, WIDE), F32),
-        pltpu.VMEM((5, NLEV * rows, WIDE), F32),
+        pltpu.VMEM((3, rows, WIDE), F32),
+        pltpu.VMEM((6, NLEV * rows, WIDE), F32),
         pltpu.VMEM((72 * 8, lanes), F32),
         pltpu.VMEM((72, lanes), F32),
         pltpu.VMEM((NG, lanes), F32),
@@ -335,7 +349,7 @@
     def pieces(first):
         got = []
         for i in range(5):
-            rows = pl.ds(NLEV - 8, 8) if first else pl.ds(0, NLEV - 8)
+            rows = pl.ds(0, 8) if first else pl.ds(8, NLEV - 8)
             src, dst = (r.at[rows] if i == 4 else r.at[:, rows] for r in (big[i], local[i]))
             got.append(pltpu.make_async_copy(src, dst, in_sem.at[i if first else 5 + i]))
         if first:
@@ -383,7 +397,7 @@
             ).start()
         recv[me] = send[me]
 
-    h, _ = physics(Tile(0, True), local + small, scr, loaded=loaded, midway=midway, after_up=ship)
+    h, _ = physics(Tile(0, True), local + small, scr, loaded=loaded, midway=midway, after_down=ship)
     heat[...] = h + jnp.where(many, heat0[...], 0.0)
     rest = recv.at[pl.ds(0, DEVS - 1)]
     pltpu.make_async_copy(rest, rest, recv_sem).wait()
@@ -395,6 +409,14 @@
     at, s = iota((DEVS, CH), 0), iota((DEVS, CH), 1)
     surface[...] = jnp.sum(jnp.where(s // 2 == at, jnp.where(s % 2 == 0, even, odd), 0.0), axis=0, keepdims=True)
     pltpu.make_async_copy(rest, rest, send_sem).wait()
+
+
+def store_kernel(heat, surface, heat_out, surface_out, sem):
+    copies = [pltpu.make_async_copy(heat, heat_out, sem.at[0]), pltpu.make_async_copy(surface, surface_out, sem.at[1])]
+    for copy in copies:
+        copy.start()
+    for copy in copies:
+        copy.wait()
 
 
 def farthest_first(e, c):
@@ -444,6 +466,14 @@
         + scratch(Tile(0, True)),
         compiler_params=pltpu.CompilerParams(vmem_limit_bytes=LIMIT, collective_id=0, has_side_effects=True),
     )(*args, *extra)
+    heat, surface = pl.pallas_call(
+        store_kernel,
+        out_shape=outs,
+        in_specs=[vmem, vmem],
+        out_specs=(hbm, hbm),
+        scratch_shapes=[pltpu.SemaphoreType.DMA((2,))],
+        compiler_params=pltpu.CompilerParams(vmem_limit_bytes=2 * 2**20),
+    )(heat, surface)
     return heat, surface.reshape(CH)
 
 

time: 30.7 us -> 28.8 us (0.938)
  local copies, waits for them, and re-layouts: 1.19 us -> 0 us
  Pallas kernels: 28.7 us -> 27.9 us
    pallas_call x1, Pallas kernels: 27.8 us -> 26.4 us  [body(): pl.pallas_call(main_kernel, out_shape=(pltpu.VMEM((NLEV, CH), F32), pltpu...]
    unnamed x2 -> x0, local copies, waits for them, and re-layouts: 1.19 us -> none
    pallas_call x0 -> x1, Pallas kernels: none -> 0.65 us  [body(): pl.pallas_call(store_kernel, out_shape=outs, in_specs=[vmem, vmem], out_s...]
where the time goes in v2:
time: 28.8 us; the launch traced here: 28.6 us
  Pallas kernels  27.9 us (97%)
  between operations  0.64 us (2%)
    pallas_call x1, Pallas kernels, body(): pl.pallas_call(main_kernel, out_shape=(pltpu.VMEM((NLEV, CH), F32), pltpu...  26.4 us
    pallas_call x1, Pallas kernels, body(): pl.pallas_call(overflow_kernel, out_shape=outs, in_specs=[vmem] + [hbm] *...  0.93 us
    pallas_call x1, Pallas kernels, body(): pl.pallas_call(store_kernel, out_shape=outs, in_specs=[vmem, vmem], out_s...  0.65 us

profile of v2, /device:TPU:1, one launch (start us, length us, event | category | flops | bytes accessed | tf_op | source)
XLA Modules:
  0.0 28.6 jit_solution(15800152428523593317)
XLA Ops:
  0.6 0.9 %shard_map.131 = (f32[64,256]{1,0:T(8,128)}, f32[1,256]{1,0:T(1,128)}) custom-call(s32[1,256]{1,0:T(1,128)} %bitcast.7, f32[8,64,256]{2,1,0:T(8,128)} %refs_0_.1, f32[14,64,256]{2,1,0:T(8,128)} %refs_1_.3, f32[14,64,256]{2,1,0:T(8,128)} %refs_2_.3, f32[14,64,256]{2,1,0:T(8,128)} %refs_3_.3, f32[64,256]{1,0:T(8,128)} %refs_4_.3, f32[1,256]{1,0:T(1,128)} %bitcast.5, ...), custom_call_target="tpu_custom_call" | custom-call | tf_op jit(solution)/shard_map/pallas_call | solution.py:441
  1.6 26.4 %shard_map.132 = (f32[64,256]{1,0:T(8,128)S(1)}, f32[1,256]{1,0:T(1,128)S(1)}) custom-call(f32[8,64,256]{2,1,0:T(8,128)} %refs_0_.1, f32[14,64,256]{2,1,0:T(8,128)} %refs_1_.3, f32[14,64,256]{2,1,0:T(8,128)} %refs_2_.3, f32[14,64,256]{2,1,0:T(8,128)} %refs_3_.3, f32[64,256]{1,0:T(8,128)} %refs_4_.3, f32[1,256]{1,0:T(1,128)} %bitcast.6, f32[14,256]{1,0:T(8,128)} %refs_6_.1, ...), custom_call_target="tpu_custom_call" | custom-call | tf_op jit(solution)/shard_map/pallas_call | solution.py:451
  27.9 0.7 %shard_map.133 = (f32[64,256]{1,0:T(8,128)}, f32[1,256]{1,0:T(1,128)}) custom-call(f32[64,256]{1,0:T(8,128)S(1)} %get-tuple-element.10.heat, f32[1,256]{1,0:T(1,128)S(1)} %get-tuple-element.11.surface), custom_call_target="tpu_custom_call" | custom-call | tf_op jit(solution)/shard_map/pallas_call | solution.py:469

commit v3 on v2

--- a/solution.py
+++ b/solution.py
@@ -338,11 +338,11 @@
 
 
 def main_kernel(*refs):
-    big, (mu, alb_hbm, sun, slot, kc_hbm, sol, band) = refs[:5], refs[5:12]
-    heat0_hbm, slotted0, (heat, surface) = refs[12], refs[13], refs[14:16]
+    big, (mu_hbm, alb_hbm, sun_hbm, slot_hbm, kc_hbm, sol_hbm, band_hbm) = refs[:5], refs[5:12]
+    heat0_hbm, slotted0_hbm, (heat, surface) = refs[12], refs[13], refs[14:16]
     send, recv, heat0, send_sem, recv_sem, go, in_sem = refs[16:23]
-    local, alb, kc, scr = refs[23:28], refs[28], refs[29], refs[30:]
-    small = (mu, alb, sun, slot, kc, sol, band)
+    local, small, slotted0, scr = refs[23:28], refs[28:35], refs[35], refs[36:]
+    mu, alb, sun, slot, kc, sol, band = small
     e, c = lax.axis_index("elem"), lax.axis_index("col")
     me = e * N_COL + c
 
@@ -357,11 +357,13 @@
             got.append(pltpu.make_async_copy(kc_hbm, kc, in_sem.at[12]))
         else:
             got.append(pltpu.make_async_copy(heat0_hbm, heat0, in_sem.at[10]))
+            got.append(pltpu.make_async_copy(slotted0_hbm, slotted0, in_sem.at[18]))
         return got
 
-    for first in (True, False):
-        for copy in pieces(first):
-            copy.start()
+    tiny = [(sun_hbm, sun), (slot_hbm, slot), (mu_hbm, mu), (sol_hbm, sol), (band_hbm, band)]
+    tiny = [pltpu.make_async_copy(src, dst, in_sem.at[13 + i]) for i, (src, dst) in enumerate(tiny)]
+    for copy in tiny + pieces(True) + pieces(False):
+        copy.start()
 
     barrier = pltpu.get_barrier_semaphore()
     for k in range(1, N_COL):
@@ -378,6 +380,8 @@
         for k in range(1, N_ELEM):
             pl.semaphore_signal(go, inc=1, device_id=(lax.rem(e + k, N_ELEM), c), device_id_type=MESH)
 
+    for copy in tiny:
+        copy.wait()
     many = jnp.sum(jnp.where(sun[...] == 1, 1.0, 0.0), axis=1, keepdims=True) > MAIN
 
     def ship(slotted):
@@ -451,7 +455,7 @@
     heat, surface = pl.pallas_call(
         main_kernel,
         out_shape=(pltpu.VMEM((NLEV, CH), F32), pltpu.VMEM((1, CH), F32)),
-        in_specs=[hbm] * 5 + [vmem, hbm, vmem, vmem, hbm, vmem, vmem] + [hbm, vmem],
+        in_specs=[hbm] * 14,
         out_specs=(vmem, vmem),
         scratch_shapes=[
             pltpu.VMEM((DEVS, 1, 128), F32),
@@ -460,9 +464,10 @@
             pltpu.SemaphoreType.DMA,
             pltpu.SemaphoreType.DMA,
             pltpu.SemaphoreType.REGULAR,
-            pltpu.SemaphoreType.DMA((13,)),
+            pltpu.SemaphoreType.DMA((19,)),
         ]
-        + [pltpu.VMEM(a.shape, a.dtype) for a in args[:5] + (args[6], args[9])]
+        + [pltpu.VMEM(a.shape, a.dtype) for a in args]
+        + [pltpu.VMEM((1, CH), F32)]
         + scratch(Tile(0, True)),
         compiler_params=pltpu.CompilerParams(vmem_limit_bytes=LIMIT, collective_id=0, has_side_effects=True),
     )(*args, *extra)

time: 28.8 us -> 27.8 us (0.965)
  Pallas kernels: 27.9 us -> 27 us
    pallas_call x1, Pallas kernels: 26.4 us -> 25.4 us  [body(): pl.pallas_call(main_kernel, out_shape=(pltpu.VMEM((NLEV, CH), F32), pltpu...]
where the time goes in v3:
time: 27.8 us; the launch traced here: 27.6 us
  Pallas kernels  27 us (97%)
  between operations  0.64 us (2%)
    pallas_call x1, Pallas kernels, body(): pl.pallas_call(main_kernel, out_shape=(pltpu.VMEM((NLEV, CH), F32), pltpu...  25.4 us
    pallas_call x1, Pallas kernels, body(): pl.pallas_call(overflow_kernel, out_shape=outs, in_specs=[vmem] + [hbm] *...  0.93 us
    pallas_call x1, Pallas kernels, body(): pl.pallas_call(store_kernel, out_shape=outs, in_specs=[vmem, vmem], out_s...  0.65 us

profile of v3, /device:TPU:1, one launch (start us, length us, event | category | flops | bytes accessed | tf_op | source)
XLA Modules:
  0.0 27.6 jit_solution(1909703532355138597)
XLA Ops:
  0.6 0.9 %shard_map.131 = (f32[64,256]{1,0:T(8,128)}, f32[1,256]{1,0:T(1,128)}) custom-call(s32[1,256]{1,0:T(1,128)} %bitcast.7, f32[8,64,256]{2,1,0:T(8,128)} %refs_0_.1, f32[14,64,256]{2,1,0:T(8,128)} %refs_1_.3, f32[14,64,256]{2,1,0:T(8,128)} %refs_2_.3, f32[14,64,256]{2,1,0:T(8,128)} %refs_3_.3, f32[64,256]{1,0:T(8,128)} %refs_4_.3, f32[1,256]{1,0:T(1,128)} %bitcast.5, ...), custom_call_target="tpu_custom_call" | custom-call | tf_op jit(solution)/shard_map/pallas_call | solution.py:445
  1.6 25.4 %shard_map.132 = (f32[64,256]{1,0:T(8,128)S(1)}, f32[1,256]{1,0:T(1,128)S(1)}) custom-call(f32[8,64,256]{2,1,0:T(8,128)} %refs_0_.1, f32[14,64,256]{2,1,0:T(8,128)} %refs_1_.3, f32[14,64,256]{2,1,0:T(8,128)} %refs_2_.3, f32[14,64,256]{2,1,0:T(8,128)} %refs_3_.3, f32[64,256]{1,0:T(8,128)} %refs_4_.3, f32[1,256]{1,0:T(1,128)} %bitcast.6, f32[14,256]{1,0:T(8,128)} %refs_6_.1, ...), custom_call_target="tpu_custom_call" | custom-call | tf_op jit(solution)/shard_map/pallas_call | solution.py:455
  27.0 0.7 %shard_map.133 = (f32[64,256]{1,0:T(8,128)}, f32[1,256]{1,0:T(1,128)}) custom-call(f32[64,256]{1,0:T(8,128)S(1)} %get-tuple-element.10.heat, f32[1,256]{1,0:T(1,128)S(1)} %get-tuple-element.11.surface), custom_call_target="tpu_custom_call" | custom-call | tf_op jit(solution)/shard_map/pallas_call | solution.py:474

commit v4 on v3

--- a/solution.py
+++ b/solution.py
@@ -244,12 +244,15 @@
             pl.when(i == 5)(midway)
         optics(1)
         descend(grp, 0)
-        prepare(jnp.minimum(grp + 1, 7))
+        prepare(grp + 1)
         optics(0)
         descend(grp, 1)
         return 0
 
-    lax.fori_loop(0, 8, downward, 0)
+    lax.fori_loop(0, 7, downward, 0)
+    optics(1)
+    descend(7, 0)
+    descend(7, 1)
 
     def side(make):
         parts = [sum(make(c) for c in range(A_CHUNKS))]

time: 27.8 us -> 27.4 us (0.986)
  Pallas kernels: 27 us -> 26.7 us
    pallas_call x1, Pallas kernels: 25.4 us -> 25.1 us  [body(): pl.pallas_call(main_kernel, out_shape=(pltpu.VMEM((NLEV, CH), F32), pltpu...]
where the time goes in v4:
time: 27.4 us; the launch traced here: 27.3 us
  Pallas kernels  26.7 us (97%)
  between operations  0.64 us (2%)
    pallas_call x1, Pallas kernels, body(): pl.pallas_call(main_kernel, out_shape=(pltpu.VMEM((NLEV, CH), F32), pltpu...  25.1 us
    pallas_call x1, Pallas kernels, body(): pl.pallas_call(overflow_kernel, out_shape=outs, in_specs=[vmem] + [hbm] *...  0.93 us
    pallas_call x1, Pallas kernels, body(): pl.pallas_call(store_kernel, out_shape=outs, in_specs=[vmem, vmem], out_s...  0.65 us

profile of v4, /device:TPU:1, one launch (start us, length us, event | category | flops | bytes accessed | tf_op | source)
XLA Modules:
  0.0 27.3 jit_solution(2028589476462245122)
XLA Ops:
  0.6 0.9 %shard_map.131 = (f32[64,256]{1,0:T(8,128)}, f32[1,256]{1,0:T(1,128)}) custom-call(s32[1,256]{1,0:T(1,128)} %bitcast.7, f32[8,64,256]{2,1,0:T(8,128)} %refs_0_.1, f32[14,64,256]{2,1,0:T(8,128)} %refs_1_.3, f32[14,64,256]{2,1,0:T(8,128)} %refs_2_.3, f32[14,64,256]{2,1,0:T(8,128)} %refs_3_.3, f32[64,256]{1,0:T(8,128)} %refs_4_.3, f32[1,256]{1,0:T(1,128)} %bitcast.5, ...), custom_call_target="tpu_custom_call" | custom-call | tf_op jit(solution)/shard_map/pallas_call | solution.py:448
  1.6 25.1 %shard_map.132 = (f32[64,256]{1,0:T(8,128)S(1)}, f32[1,256]{1,0:T(1,128)S(1)}) custom-call(f32[8,64,256]{2,1,0:T(8,128)} %refs_0_.1, f32[14,64,256]{2,1,0:T(8,128)} %refs_1_.3, f32[14,64,256]{2,1,0:T(8,128)} %refs_2_.3, f32[14,64,256]{2,1,0:T(8,128)} %refs_3_.3, f32[64,256]{1,0:T(8,128)} %refs_4_.3, f32[1,256]{1,0:T(1,128)} %bitcast.6, f32[14,256]{1,0:T(8,128)} %refs_6_.1, ...), custom_call_target="tpu_custom_call" | custom-call | tf_op jit(solution)/shard_map/pallas_call | solution.py:458
  26.7 0.7 %shard_map.133 = (f32[64,256]{1,0:T(8,128)}, f32[1,256]{1,0:T(1,128)}) custom-call(f32[64,256]{1,0:T(8,128)S(1)} %get-tuple-element.10.heat, f32[1,256]{1,0:T(1,128)S(1)} %get-tuple-element.11.surface), custom_call_target="tpu_custom_call" | custom-call | tf_op jit(solution)/shard_map/pallas_call | solution.py:477
